TPU v7x, 256 devices: a whole 4x4x8 slice. The times are simulated.
256 devices in a mesh: seq: 64 (over y, z, core), chan: 4 (over x).
Axes of the slice: x: 4, y: 4, z: 8, core: 2. Of those that a mesh axis runs over, the one named last changes fastest.
Arguments:
- inputs: bfloat16 [8192, 4096], P('seq', 'chan'), may hold values from -6 to 6
- grads: bfloat16 [8192, 4096], P('seq', 'chan'), may hold values from -0.15625 to 0.15625
- filter_taps: float32 [512, 4096], P(('seq', 'chan')), may hold values from -6 to 6
- supports: int32 [32], replicated, may hold values from 1 to 4, as said below
Outputs:
- grad_inputs: bfloat16 [8192, 4096], P('seq', 'chan')
- grad_filter: float32 [512, 4096], P(('seq', 'chan'))
Inputs may be any that keep to these rules, and one draw needn't show every extreme that they name: `supports`: some group spans 4 blocks and some group spans 1 block.
All inputs are finite; a program needn't handle non-finite values.
Results may differ from a plain program's by a relative error of at most 0.001.
Values may be sent and summed in bfloat16 or wider, within the bound.
A program may use at most 64 MiB of HBM per device.

v0:
```python
import math

import jax
import jax.numpy as jnp
from jax import lax
from jax.sharding import PartitionSpec as P

GROUP_CH = 128


HIGHEST = lax.Precision.HIGHEST


def passed_along(value, axis, by):
    length = lax.axis_size(axis)
    pairs = [(i, i + by) for i in range(length) if 0 <= i + by < length]
    return lax.ppermute(value, axis, pairs)


def fourier_tables(span_len, block_len):
    index = jnp.arange(span_len, dtype=jnp.int32)
    phase = index[:, None] * index[None, :] % span_len
    angles = phase.astype(jnp.float32) * (2.0 * math.pi / span_len)
    cosine = jnp.cos(angles)
    sine = jnp.sin(angles)
    forward_full = jnp.concatenate([cosine, -sine], axis=0)
    forward_half = forward_full[:, :block_len]
    inverse = jnp.concatenate([cosine, -sine], axis=1) / span_len
    return (forward_full, forward_half, inverse)


def apply_table(table, values):
    return jnp.dot(table, values, precision=HIGHEST, preferred_element_type=jnp.float32)


def times_conj(first, second, half):
    first_re, first_im = (first[:half], first[half:])
    second_re, second_im = (second[:half], second[half:])
    real_part = first_re * second_re + first_im * second_im
    imag_part = first_im * second_re - first_re * second_im
    return jnp.concatenate([real_part, imag_part], axis=0)


def body(inputs, grads, filter_taps, supports):
    block_len, width_here = inputs.shape
    span_len = 2 * block_len
    chan_index = lax.axis_index("chan")
    seq_count = lax.axis_size("seq")
    reach = max(2, seq_count // 16)
    lag_total = reach * block_len
    groups_here = width_here // GROUP_CH
    own_support = lax.dynamic_slice_in_dim(supports, chan_index * groups_here, groups_here, 0)
    limit = jnp.repeat(own_support, GROUP_CH) * block_len
    lag_pos = jnp.arange(lag_total, dtype=jnp.int32)[:, None]
    own_taps = lax.all_to_all(filter_taps, "chan", split_axis=1, concat_axis=0, tiled=True)
    all_taps = lax.all_gather(own_taps, "seq", axis=0, tiled=True)
    all_taps = jnp.where(lag_pos < limit[None, :], all_taps, 0.0)
    padded_taps = jnp.pad(all_taps, ((block_len, block_len), (0, 0)))
    forward_full, forward_half, inverse = fourier_tables(span_len, block_len)
    own_grad_spec = apply_table(forward_half, grads.astype(jnp.float32))
    window_list = []
    for offset in range(reach + 1):
        window = padded_taps[offset * block_len : offset * block_len + span_len]
        circular = jnp.concatenate([window[block_len:], window[:block_len]], axis=0)
        window_list.append(apply_table(forward_full, circular))
    window_specs = jnp.stack(window_list, axis=0)

    def pair_update(step, signal_blk, upstream_blk, lag_sums, input_spec):
        signal_spec = apply_table(forward_half, signal_blk.astype(jnp.float32))
        upstream_spec = apply_table(forward_half, upstream_blk.astype(jnp.float32))
        window_spec = lax.dynamic_index_in_dim(window_specs, step, 0, keepdims=False)
        corr = apply_table(inverse, times_conj(own_grad_spec, signal_spec, span_len))
        shifted = jnp.concatenate([corr[block_len:], corr[:block_len]], axis=0)
        current = lax.dynamic_slice_in_dim(lag_sums, step * block_len, span_len, 0)
        lag_sums = lax.dynamic_update_slice_in_dim(lag_sums, current + shifted, step * block_len, 0)
        input_spec = input_spec + times_conj(upstream_spec, window_spec, span_len)
        return (lag_sums, input_spec)

    lag_sums = jnp.zeros(((reach + 2) * block_len, width_here), jnp.float32)
    input_spec = jnp.zeros((2 * span_len, width_here), jnp.float32)
    lag_sums, input_spec = pair_update(0, inputs, grads, lag_sums, input_spec)

    def passed_step(step, carry):
        signal_now, upstream_now, sums_now, spec_now = carry
        signal_now = passed_along(signal_now, "seq", 1)
        upstream_now = passed_along(upstream_now, "seq", -1)
        sums_now, spec_now = pair_update(step, signal_now, upstream_now, sums_now, spec_now)
        return (signal_now, upstream_now, sums_now, spec_now)

    carried = lax.fori_loop(1, reach + 1, passed_step, (inputs, grads, lag_sums, input_spec))
    lag_sums, input_spec = (carried[2], carried[3])
    grad_inputs = apply_table(inverse[:block_len], input_spec).astype(jnp.bfloat16)
    filter_term = lag_sums[block_len : block_len + lag_total]
    filter_term = jnp.where(lag_pos < limit[None, :], filter_term, 0.0)
    owned = lax.psum_scatter(filter_term, "seq", scatter_dimension=0, tiled=True)
    grad_filter = lax.all_to_all(owned, "chan", split_axis=0, concat_axis=1, tiled=True)
    return (grad_inputs, grad_filter)


def solution(mesh):
    in_specs = (P("seq", "chan"), P("seq", "chan"), P(("seq", "chan"), None), P())
    out_specs = (P("seq", "chan"), P(("seq", "chan"), None))
    return jax.shard_map(body, mesh=mesh, in_specs=in_specs, out_specs=out_specs, check_vma=False)
```

profile of v0, /device:TPU:1, one launch (start us, length us, event | category | flops | bytes accessed | tf_op | source)
XLA Modules:
  0.0 364.4 jit_solution(2163823448418783979)
XLA Ops:
  7.2 1.7 copy.33
  8.9 1.7 copy.32
  10.5 9.1 %all_to_all.38 = f32[2,4,1024]{2,0,1:T(2,128)S(1)} all-to-all(f32[2,4,1024]{2,0,1:T(2,128)} %bitcast.71), channel_id=1, replica_groups=mesh['seq'=64,'chan'=4] {'chan'}, dimensions={1} | all-to-all | bytes 65536 | tf_op jit(solution)/shard_map/all_to_all | solution.py:55
  23.4 3.3 fusion.48
  26.7 74.1 %all-gather.2.cloned.1.call-done = f32[512,1024]{1,0:T(8,128)} async-done(((f32[8,1024]{1,0:T(8,128)}), f32[512,1024]{1,0:T(8,128)}) %all-gather.2.cloned.1.call-update) | async-done | bytes 2097168 | tf_op jit(solution)/shard_map/all_gather | solution.py:56
  100.8 1.8 fusion.13
  103.3 3.3 constant_dynamic-update-slice_fusion
  106.6 3.2 bitcast_dynamic-update-slice_fusion.3
  109.8 3.2 bitcast_dynamic-update-slice_fusion.2
  113.0 3.2 bitcast_dynamic-update-slice_fusion.1
  116.2 3.4 bitcast_dynamic-update-slice_fusion
  120.6 1.9 fusion.9
  122.6 1.6 pad_maximum_fusion
  124.2 2.2 select_maximum_fusion
  126.4 75.9 %while.21 = (s32[]{:T(128)}, bf16[128,1024]{1,0:T(8,128)(2,1)}, bf16[128,1024]{1,0:T(8,128)(2,1)}, f32[768,1024]{1,0:T(8,128)}, f32[512,1024]{1,0:T(8,128)}, /*i...) while((s32[]{:T(128)}, bf16[128,1024]{1,0:T(8,128)(2,1)}, ...), condition=%wide.region_1.2_spmd, body=%wide.region_0.1_spmd.sunk | while | flops 3226468352 | bytes 78119352 | solution.py:90
  126.4 2.4 collective-permute-start
  128.8 2.0 collective-permute-start.1
  130.7 1.6 collective-permute-done
  133.8 2.0 fusion.77
  137.6 2.1 multiply_add_fusion.7
  140.5 1.8 copy-done.3
  143.3 1.2 copy.26
  144.5 3.5 collective-permute-start
  148.0 1.9 collective-permute-start.1
  150.0 1.7 collective-permute-done
  153.1 2.0 fusion.77
  156.9 2.1 multiply_add_fusion.7
  159.8 1.8 copy-done.3
  162.6 1.2 copy.26
  163.7 3.5 collective-permute-start
  167.3 1.9 collective-permute-start.1
  169.2 1.7 collective-permute-done
  172.3 2.0 fusion.77
  176.2 2.1 multiply_add_fusion.7
  179.1 1.8 copy-done.3
  181.8 1.2 copy.26
  183.0 3.5 collective-permute-start
  186.6 1.9 collective-permute-start.1
  188.5 1.7 collective-permute-done
  191.6 2.0 fusion.77
  195.4 2.1 multiply_add_fusion.7
  198.3 1.8 copy-done.3
  202.3 3.4 slice_select_fusion
  205.7 141.6 %reduce-scatter.2.cloned.1.call-done = f32[8,1024]{1,0:T(8,128)} async-done(((f32[512,1024]{1,0:T(8,128)}), f32[8,1024]{1,0:T(8,128)}) %reduce-scatter.2.cloned.1.call-update) | async-done | bytes 32784 | tf_op jit(solution)/shard_map/reduce_scatter | solution.py:95
  347.3 1.4 all_to_all.32
  348.7 3.9 %all-to-all-start.1 = ((f32[4,2,1024]{2,1,0:T(2,128)}), f32[4,2,1024]{2,1,0:T(2,128)S(1)}, u32[]{:S(2)}, u32[]{:S(2)}) async-start(f32[4,2,1024]{2,1,0:T(2,128)} %all_to_all.32), calls=%async_computation.2 | async-start | bytes 65536 | tf_op jit(solution)/shard_map/all_to_all | solution.py:96
  352.7 2.0 convolution_convert_fusion
  354.6 2.3 all-to-all-done.1
  (84 shorter events, 26.9 us)
Async XLA Ops:
  7.2 93.6 %all-gather.2.cloned.1.call-start = ((), (), s32[]{:S(2)}) async-start(), calls=%async_computation.3 | async-start | bytes 2129920 | tf_op jit(solution)/shard_map/all_gather | solution.py:56
  20.3 327.0 %reduce-scatter.2.cloned.1.call-start = ((), (), s32[]{:S(2)}) async-start(), calls=%async_computation.4 | async-start | bytes 2129920 | tf_op jit(solution)/shard_map/reduce_scatter | solution.py:95
  20.4 2.0 copy-start.6
  102.6 0.7 copy-start.7
  116.2 3.4 copy-start.5
  126.4 6.0 %collective-permute-start = (bf16[128,1024]{1,0:T(8,128)(2,1)}, bf16[128,1024]{1,0:T(8,128)(2,1)S(1)}, u32[]{:S(2)}, u32[]{:S(2)}) collective-permute-start(bf16[128,1024]{1,0:T(8,128)(2,1)} %get-tuple-element.348), channel_id=1, source_target_pairs={{0,4},{4,8},{8,12},{12,16},{16,20},{20,24},{24,28},{28,32},{32,36}... | collective-permute-start | bytes 786440 | tf_op jit(solution)/shard_map/while/body/eval_jaxpr/ppermute | solution.py:17
  128.8 7.9 %collective-permute-start.1 = (bf16[128,1024]{1,0:T(8,128)(2,1)}, bf16[128,1024]{1,0:T(8,128)(2,1)S(1)}, u32[]{:S(2)}, u32[]{:S(2)}) collective-permute-start(bf16[128,1024]{1,0:T(8,128)(2,1)} %get-tuple-element.349), channel_id=1, source_target_pairs={{4,0},{8,4},{12,8},{16,12},{20,16},{24,20},{28,24},{32,28},{36,32}... | collective-permute-start | bytes 786440 | tf_op jit(solution)/shard_map/while/body/eval_jaxpr/ppermute | solution.py:17
  137.6 2.2 copy-start
  139.9 2.5 copy-start.3
  140.5 3.9 %copy-start.1 = (f32[512,1024]{1,0:T(8,128)}, f32[512,1024]{1,0:T(8,128)S(1)}, u32[]{:S(2)}) copy-start(f32[512,1024]{1,0:T(8,128)S(1)} %maximum_add_fusion.3) | copy-start | bytes 6291460 | tf_op jit(solution)/shard_map/while
  142.6 1.9 copy-start.4
  144.5 7.2 %collective-permute-start = (bf16[128,1024]{1,0:T(8,128)(2,1)}, bf16[128,1024]{1,0:T(8,128)(2,1)S(1)}, u32[]{:S(2)}, u32[]{:S(2)}) collective-permute-start(bf16[128,1024]{1,0:T(8,128)(2,1)} %get-tuple-element.348), channel_id=1, source_target_pairs={{0,4},{4,8},{8,12},{12,16},{16,20},{20,24},{24,28},{28,32},{32,36}... | collective-permute-start | bytes 786440 | tf_op jit(solution)/shard_map/while/body/eval_jaxpr/ppermute | solution.py:17
  148.0 7.9 %collective-permute-start.1 = (bf16[128,1024]{1,0:T(8,128)(2,1)}, bf16[128,1024]{1,0:T(8,128)(2,1)S(1)}, u32[]{:S(2)}, u32[]{:S(2)}) collective-permute-start(bf16[128,1024]{1,0:T(8,128)(2,1)} %get-tuple-element.349), channel_id=1, source_target_pairs={{4,0},{8,4},{12,8},{16,12},{20,16},{24,20},{28,24},{32,28},{36,32}... | collective-permute-start | bytes 786440 | tf_op jit(solution)/shard_map/while/body/eval_jaxpr/ppermute | solution.py:17
  156.9 2.2 copy-start
  159.1 2.5 copy-start.3
  159.8 3.9 %copy-start.1 = (f32[512,1024]{1,0:T(8,128)}, f32[512,1024]{1,0:T(8,128)S(1)}, u32[]{:S(2)}) copy-start(f32[512,1024]{1,0:T(8,128)S(1)} %maximum_add_fusion.3) | copy-start | bytes 6291460 | tf_op jit(solution)/shard_map/while
  161.8 1.9 copy-start.4
  163.7 7.2 %collective-permute-start = (bf16[128,1024]{1,0:T(8,128)(2,1)}, bf16[128,1024]{1,0:T(8,128)(2,1)S(1)}, u32[]{:S(2)}, u32[]{:S(2)}) collective-permute-start(bf16[128,1024]{1,0:T(8,128)(2,1)} %get-tuple-element.348), channel_id=1, source_target_pairs={{0,4},{4,8},{8,12},{12,16},{16,20},{20,24},{24,28},{28,32},{32,36}... | collective-permute-start | bytes 786440 | tf_op jit(solution)/shard_map/while/body/eval_jaxpr/ppermute | solution.py:17
  167.3 7.9 %collective-permute-start.1 = (bf16[128,1024]{1,0:T(8,128)(2,1)}, bf16[128,1024]{1,0:T(8,128)(2,1)S(1)}, u32[]{:S(2)}, u32[]{:S(2)}) collective-permute-start(bf16[128,1024]{1,0:T(8,128)(2,1)} %get-tuple-element.349), channel_id=1, source_target_pairs={{4,0},{8,4},{12,8},{16,12},{20,16},{24,20},{28,24},{32,28},{36,32}... | collective-permute-start | bytes 786440 | tf_op jit(solution)/shard_map/while/body/eval_jaxpr/ppermute | solution.py:17
  176.2 2.2 copy-start
  178.4 2.5 copy-start.3
  179.1 3.9 %copy-start.1 = (f32[512,1024]{1,0:T(8,128)}, f32[512,1024]{1,0:T(8,128)S(1)}, u32[]{:S(2)}) copy-start(f32[512,1024]{1,0:T(8,128)S(1)} %maximum_add_fusion.3) | copy-start | bytes 6291460 | tf_op jit(solution)/shard_map/while
  181.1 1.9 copy-start.4
  183.0 7.2 %collective-permute-start = (bf16[128,1024]{1,0:T(8,128)(2,1)}, bf16[128,1024]{1,0:T(8,128)(2,1)S(1)}, u32[]{:S(2)}, u32[]{:S(2)}) collective-permute-start(bf16[128,1024]{1,0:T(8,128)(2,1)} %get-tuple-element.348), channel_id=1, source_target_pairs={{0,4},{4,8},{8,12},{12,16},{16,20},{20,24},{24,28},{28,32},{32,36}... | collective-permute-start | bytes 786440 | tf_op jit(solution)/shard_map/while/body/eval_jaxpr/ppermute | solution.py:17
  186.6 7.9 %collective-permute-start.1 = (bf16[128,1024]{1,0:T(8,128)(2,1)}, bf16[128,1024]{1,0:T(8,128)(2,1)S(1)}, u32[]{:S(2)}, u32[]{:S(2)}) collective-permute-start(bf16[128,1024]{1,0:T(8,128)(2,1)} %get-tuple-element.349), channel_id=1, source_target_pairs={{4,0},{8,4},{12,8},{16,12},{20,16},{24,20},{28,24},{32,28},{36,32}... | collective-permute-start | bytes 786440 | tf_op jit(solution)/shard_map/while/body/eval_jaxpr/ppermute | solution.py:17
  195.4 2.2 copy-start
  197.7 2.5 copy-start.3
  198.3 3.9 %copy-start.1 = (f32[512,1024]{1,0:T(8,128)}, f32[512,1024]{1,0:T(8,128)S(1)}, u32[]{:S(2)}) copy-start(f32[512,1024]{1,0:T(8,128)S(1)} %maximum_add_fusion.3) | copy-start | bytes 6291460 | tf_op jit(solution)/shard_map/while
  200.4 1.9 copy-start.4
  205.7 147.0 %copy-start.2 = (f32[512,1024]{1,0:T(8,128)S(1)}, f32[512,1024]{1,0:T(8,128)}, u32[]{:S(2)}) copy-start(f32[512,1024]{1,0:T(8,128)} %get-tuple-element.223) | copy-start | bytes 6291460
  348.7 8.2 %all-to-all-start.1 = ((f32[4,2,1024]{2,1,0:T(2,128)}), f32[4,2,1024]{2,1,0:T(2,128)S(1)}, u32[]{:S(2)}, u32[]{:S(2)}) async-start(f32[4,2,1024]{2,1,0:T(2,128)} %all_to_all.32), calls=%async_computation.2 | async-start | bytes 65536 | tf_op jit(solution)/shard_map/all_to_all | solution.py:96
Sparse Core Ops, SparseCore 0:
  20.5 80.2 all-gather.1
  205.8 141.4 reduce-scatter.1
where the time goes:
time: 370 us; the launch traced here: 364 us
  waiting for transfers between devices  228 us (62%)
  matrix products  40.2 us (11%)
  other arithmetic  25.6 us (7%)
  starting transfers between devices  24.7 us (7%)
  local copies, waits for them, and re-layouts  22.4 us (6%)
  between operations  14.1 us (4%)
  blocking collectives  9.14 us (2%)
    reduce_scatter x1, waiting for transfers between devices, body(): lax.psum_scatter(filter_term, 'seq', scatter_dimension=0, tiled=True)  142 us
    all_gather x1, waiting for transfers between devices, body(): all_taps = lax.all_gather(own_taps, 'seq', axis=0, tiled=True)  74.1 us
    dot_general x21, matrix products, apply_table(): jnp.dot(table, values, precision=HIGHEST, preferred_element_type=jnp.floa...  40.2 us
    ppermute x8, starting transfers between devices, passed_along(): return lax.ppermute(value, axis, pairs)  20.7 us
    while x40, local copies, waits for them, and re-layouts  15.2 us
    add x9, other arithmetic, times_conj(): real_part = first_re * second_re + first_im * second_im  11.2 us
    ppermute x8, waiting for transfers between devices, passed_along(): return lax.ppermute(value, axis, pairs)  9.65 us
    all_to_all x1, blocking collectives, body(): lax.all_to_all(filter_taps, 'chan', split_axis=1, concat_axis=0, tiled=True)  9.14 us
  transfers between devices with their start and end apart: 11, of which 11 were waited for; matrix products, arithmetic and copies ran while one was open for 6% of the time, Pallas kernels for 0%

commit v1 on v0

v1 whole, which is shorter than its diff:
```python
import functools

import jax
import jax.numpy as jnp
from jax import lax
from jax.experimental import pallas as pl
from jax.experimental.pallas import tpu as pltpu
from jax.sharding import PartitionSpec as P

MESH = pl.DeviceIdType.MESH
F32 = jnp.float32
BF16 = jnp.bfloat16
TB = 128
SMAX = 4
SEQ_DEV = 64
CHAN_DEV = 4
WIDTH = 1024
OWN = 16
LAGS = SMAX * TB
SPAN = LAGS + TB
ROWS = SEQ_DEV * OWN
NT = (((1,), (1,)), ((), ()))


def iota(shape, axis):
    return lax.broadcasted_iota(jnp.int32, shape, axis)


def high_low(value):
    high = value.astype(BF16)
    return jnp.concatenate([high, (value - high.astype(F32)).astype(BF16)], axis=0)


def take_all(landed, send_sem, recv_sem, count):
    span = landed.at[pl.ds(0, count)]
    pltpu.make_async_copy(span, span, recv_sem).wait()
    pltpu.make_async_copy(span, span, send_sem).wait()


def spread(source, landed, send_sem, recv_sem, me):
    def one(step, carry):
        to = lax.rem(me + step, SEQ_DEV)
        pltpu.make_async_remote_copy(
            source.at[pl.ds(to, 1)], landed.at[pl.ds(me, 1)], send_sem, recv_sem, device_id={"seq": to}, device_id_type=MESH
        ).start()
        return carry

    lax.fori_loop(1, SEQ_DEV, one, 0)


def turn(block_ref, out_ref, backwards):
    mirror = jnp.where(iota((TB, TB), 0) + iota((TB, TB), 1) == TB - 1, 1.0, 0.0).astype(BF16)
    for tile in range(WIDTH // 128):
        flipped = block_ref[:, tile * 128 : (tile + 1) * 128].astype(F32).T.astype(BF16)
        if backwards:
            flipped = jnp.dot(flipped, mirror, preferred_element_type=F32).astype(BF16)
        out_ref[tile * 8 : (tile + 1) * 8] = flipped.reshape(8, OWN, 128)


def kernel(
    supports, grads, inputs, taps, gi_out, gf_out,
    g_here, x_here, t_here, g_send, x_send, g_land, x_land, gi_send,
    t_first, t_rows, row_send, row_land, g_wide, x_wide, gi_wide, toeplitz, windows, tap_lines, partial,
    order, back_send, back_land, last_send, last_land,
    in_sem, send_sem, recv_sem, local_sem,
):
    me, chan = lax.axis_index("seq"), lax.axis_index("chan")
    phase = lax.rem(me, 8)
    load_g = pltpu.make_async_copy(grads, g_here, in_sem.at[0])
    load_t = pltpu.make_async_copy(taps, t_here, in_sem.at[1])
    load_x = pltpu.make_async_copy(inputs, x_here, in_sem.at[2])
    load_g.start()
    load_t.start()
    load_x.start()

    barrier = pltpu.get_barrier_semaphore()

    def greet(step, carry):
        pl.semaphore_signal(barrier, inc=1, device_id={"seq": lax.rem(me + step, SEQ_DEV)}, device_id_type=MESH)
        return carry

    lax.fori_loop(1, SEQ_DEV, greet, 0)
    for step in range(1, CHAN_DEV):
        pl.semaphore_signal(barrier, inc=1, device_id={"chan": lax.rem(chan + step, CHAN_DEV)}, device_id_type=MESH)

    load_g.wait()
    turn(g_here, g_send, False)
    load_t.wait()
    pl.semaphore_wait(barrier, SEQ_DEV - 1 + CHAN_DEV - 1)

    for step in range(1, CHAN_DEV):
        to = lax.rem(chan + step, CHAN_DEV)
        pltpu.make_async_remote_copy(
            t_here.at[:, pl.ds(pl.multiple_of(to * WIDTH, WIDTH), WIDTH)], t_first.at[chan],
            send_sem.at[0], recv_sem.at[0], device_id={"chan": to}, device_id_type=MESH,
        ).start()
    spread(g_send, g_land, send_sem.at[1], recv_sem.at[1], me)
    g_land[me] = g_send[me]
    t_first[chan] = t_here[:, pl.ds(pl.multiple_of(chan * WIDTH, WIDTH), WIDTH)]
    load_x.wait()
    turn(x_here, x_send, True)
    x_land[me] = x_send[me]

    row = iota((512, 1), 0)
    group = ((row // 64) % 2) * 4 + row // 128
    lag_of = (row % 64) * 8 + ((phase + 8 - group) & 7)
    order[...] = jnp.where(iota((512, LAGS), 1) == lag_of, 1.0, 0.0).astype(BF16)
    lane_group, sublane = iota((8, 128), 1) // 16, iota((8, 128), 0)

    take_all(t_first, send_sem.at[0], recv_sem.at[0], CHAN_DEV - 1)
    for x in range(CHAN_DEV):
        t_rows[2 * x : 2 * x + 2, :] = t_first[x]
    for tile in range(8):
        block = t_rows[:, tile * 128 : (tile + 1) * 128]
        skewed = block
        for r in range(1, 8):
            skewed = jnp.where(sublane == r, pltpu.roll(block, 128 - 16 * r, axis=1), skewed)
        moved = skewed
        for k in range(1, 8):
            moved = jnp.where(lane_group == k, pltpu.roll(skewed, k, axis=0), moved)
        row_send[tile * 8 : (tile + 1) * 8, :] = moved
    spread(row_send, row_land, send_sem.at[2], recv_sem.at[2], me)
    row_land[pl.ds(me, 1), :] = row_send[pl.ds(me, 1), :]
    spread(x_send, x_land, send_sem.at[3], recv_sem.at[3], me)

    g_wide[ROWS:, :] = jnp.zeros((SMAX * OWN, 128), F32)
    own_lags = TB * supports[chan * (WIDTH // 128) + me // 8]

    take_all(row_land, send_sem.at[2], recv_sem.at[2], SEQ_DEV - 1)
    landed = row_land[...]
    flipped = jnp.concatenate([landed, pltpu.roll(landed, 64, axis=1)], axis=0).T
    placed = jnp.concatenate([flipped[16 * q : 16 * q + 16] for q in range(4)], axis=1)
    both = jnp.dot(high_low(placed), order[...], preferred_element_type=F32)
    own_taps = jnp.where(iota((OWN, LAGS), 1) < own_lags, both[:OWN] + both[OWN:], 0.0)
    tap_lines[...] = own_taps

    below = iota((TB, TB), 1) >= iota((TB, TB), 0)

    def build(c, carry):
        line = tap_lines[pl.ds(c, 1), :]
        before = jnp.zeros((TB, TB), F32)
        for j in range(SMAX + 1):
            if j < SMAX:
                now = jnp.broadcast_to(line[:, j * TB : (j + 1) * TB], (TB, TB))
                now = pltpu.roll(now, 0, axis=1, stride=1, stride_axis=0)
            else:
                now = jnp.zeros((TB, TB), F32)
            toeplitz[c, :, j * TB : (j + 1) * TB] = high_low(jnp.where(below, now, before))
            before = now
        return carry

    lax.fori_loop(0, OWN, build, 0)

    take_all(g_land, send_sem.at[1], recv_sem.at[1], SEQ_DEV - 1)
    g_wide[0:ROWS, :] = g_land[...].reshape(ROWS, 128).astype(F32)

    def signal_back(c, carry):
        for j in range(SMAX + 1):
            windows[c, :, j * TB : (j + 1) * TB] = g_wide[pl.ds(j * OWN + c, SEQ_DEV, stride=OWN), :].astype(BF16)
        both = lax.dot_general(windows[c], toeplitz[c], NT, preferred_element_type=F32)
        gi_wide[pl.ds(c, SEQ_DEV, stride=OWN), :] = both[:, :TB] + both[:, TB:]
        return carry

    lax.fori_loop(0, OWN, signal_back, 0)
    gi_send[...] = gi_wide[...].astype(BF16).reshape(SEQ_DEV, OWN, 128)
    spread(gi_send, gi_out, send_sem.at[4], recv_sem.at[4], me)
    keep = pltpu.make_async_copy(gi_send.at[pl.ds(me, 1)], gi_out.at[pl.ds(me, 1)], local_sem)
    keep.start()

    take_all(x_land, send_sem.at[3], recv_sem.at[3], SEQ_DEV - 1)
    x_wide[...] = x_land[...].reshape(ROWS, 128).astype(F32)
    inside = iota((TB, TB), 1) <= iota((TB, TB), 0)

    def lag_sums(c, carry):
        signal = x_wide[pl.ds(c, SEQ_DEV, stride=OWN), :].T.astype(BF16)
        after = None
        for j in range(SMAX, -1, -1):
            product = jnp.dot(signal, windows[c, :, j * TB : (j + 1) * TB], preferred_element_type=F32)
            now = pltpu.roll(product, 1, axis=1, stride=1, stride_axis=0)
            if j < SMAX:
                lined = jnp.where(inside, now, after)
                partial[j, pl.ds(c * 8, 8), :] = jnp.sum(lined.reshape(TB // 8, 8, TB), axis=0)
            after = now
        return carry

    lax.fori_loop(0, OWN, lag_sums, 0)
    blocks = []
    for j in range(SMAX):
        added = partial[j, pl.ds(0, OWN, stride=8), :]
        for q in range(1, 8):
            added = added + partial[j, pl.ds(q, OWN, stride=8), :]
        blocks.append(added)
    sums = jnp.concatenate(blocks, axis=1)
    sums = jnp.where(iota((OWN, LAGS), 1) < own_lags, sums, 0.0)
    both = lax.dot_general(high_low(sums), order[...], NT, preferred_element_type=F32)
    placed = both[:OWN] + both[OWN:]
    stacked = jnp.concatenate([placed[:, q * 128 : (q + 1) * 128] for q in range(4)], axis=0)
    flipped = jnp.concatenate([stacked, stacked], axis=0).T
    back_send[...] = jnp.where(iota((64, 128), 1) < 64, flipped[:64], flipped[64:])
    spread(back_send, back_land, send_sem.at[5], recv_sem.at[5], me)
    back_land[pl.ds(me, 1), :] = back_send[pl.ds(me, 1), :]
    take_all(back_land, send_sem.at[5], recv_sem.at[5], SEQ_DEV - 1)
    for tile in range(8):
        block = back_land[tile * 8 : (tile + 1) * 8, :]
        moved = block
        for k in range(1, 8):
            moved = jnp.where(lane_group == k, pltpu.roll(block, 8 - k, axis=0), moved)
        t_rows[:, tile * 128 : (tile + 1) * 128] = pltpu.roll(moved, 0, axis=1, stride=16, stride_axis=0)
    for x in range(CHAN_DEV):
        last_send[x] = t_rows[2 * x : 2 * x + 2, :]
    for step in range(1, CHAN_DEV):
        to = lax.rem(chan + step, CHAN_DEV)
        pltpu.make_async_remote_copy(
            last_send.at[to], last_land.at[chan], send_sem.at[6], recv_sem.at[6], device_id={"chan": to}, device_id_type=MESH
        ).start()
    last_land[chan] = last_send[chan]
    take_all(last_land, send_sem.at[6], recv_sem.at[6], CHAN_DEV - 1)
    for x in range(CHAN_DEV):
        gf_out[:, x * WIDTH : (x + 1) * WIDTH] = last_land[x]
    keep.wait()
    take_all(gi_out, send_sem.at[4], recv_sem.at[4], SEQ_DEV - 1)


def finish(gi_rows, gf_here, gi, gf):
    for tile in range(WIDTH // 128):
        lanes = slice(tile * 128, (tile + 1) * 128)
        gi[:, lanes] = gi_rows[lanes, :].astype(F32).T.astype(BF16)
    gf[...] = gf_here[...]


def body(inputs, grads, filter_taps, supports):
    vmem = pl.BlockSpec(memory_space=pltpu.VMEM)
    anywhere = pl.BlockSpec(memory_space=pl.ANY)
    blocks = (SEQ_DEV, OWN, 128)
    gi_rows, gf = pl.pallas_call(
        kernel,
        out_shape=(jax.ShapeDtypeStruct(blocks, BF16), jax.ShapeDtypeStruct((2, CHAN_DEV * WIDTH), F32)),
        in_specs=[pl.BlockSpec(memory_space=pltpu.SMEM), anywhere, anywhere, anywhere],
        out_specs=(anywhere, vmem),
        scratch_shapes=[
            pltpu.VMEM((TB, WIDTH), BF16),
            pltpu.VMEM((TB, WIDTH), BF16),
            pltpu.VMEM((2, CHAN_DEV * WIDTH), F32),
            pltpu.VMEM(blocks, BF16),
            pltpu.VMEM(blocks, BF16),
            pltpu.VMEM(blocks, BF16),
            pltpu.VMEM(blocks, BF16),
            pltpu.VMEM(blocks, BF16),
            pltpu.VMEM((CHAN_DEV, 2, WIDTH), F32),
            pltpu.VMEM((8, WIDTH), F32),
            pltpu.VMEM((SEQ_DEV, 128), F32),
            pltpu.VMEM((SEQ_DEV, 128), F32),
            pltpu.VMEM((ROWS + SMAX * OWN, 128), F32),
            pltpu.VMEM((ROWS, 128), F32),
            pltpu.VMEM((ROWS, 128), F32),
            pltpu.VMEM((OWN, 2 * TB, SPAN), BF16),
            pltpu.VMEM((OWN, SEQ_DEV, SPAN), BF16),
            pltpu.VMEM((OWN, LAGS), F32),
            pltpu.VMEM((SMAX, OWN * 8, TB), F32),
            pltpu.VMEM((512, LAGS), BF16),
            pltpu.VMEM((SEQ_DEV, 128), F32),
            pltpu.VMEM((SEQ_DEV, 128), F32),
            pltpu.VMEM((CHAN_DEV, 2, WIDTH), F32),
            pltpu.VMEM((CHAN_DEV, 2, WIDTH), F32),
            pltpu.SemaphoreType.DMA((3,)),
            pltpu.SemaphoreType.DMA((7,)),
            pltpu.SemaphoreType.DMA((7,)),
            pltpu.SemaphoreType.DMA,
        ],
        compiler_params=pltpu.CompilerParams(collective_id=0, has_side_effects=True, vmem_limit_bytes=48 * 2**20),
    )(supports, grads, inputs, filter_taps)
    return pl.pallas_call(
        finish,
        out_shape=(jax.ShapeDtypeStruct((TB, WIDTH), BF16), jax.ShapeDtypeStruct((2, CHAN_DEV * WIDTH), F32)),
        in_specs=[vmem, vmem],
        out_specs=(vmem, vmem),
    )(gi_rows.reshape(ROWS, 128), gf)


def solution(mesh):
    in_specs = (P("seq", "chan"), P("seq", "chan"), P(("seq", "chan"), None), P())
    out_specs = (P("seq", "chan"), P(("seq", "chan"), None))
    return jax.shard_map(body, mesh=mesh, in_specs=in_specs, out_specs=out_specs, check_vma=False)
```

time: 370 us -> 54.9 us (0.15); the launches traced: 364 us -> 54.6 us
  waiting for transfers between devices: 228 us -> 0 us
  Pallas kernels: 0 us -> 49.4 us
  matrix products: 40.2 us -> 0 us
  other arithmetic: 25.6 us -> 0 us
  starting transfers between devices: 24.7 us -> 0 us
  local copies, waits for them, and re-layouts: 22.4 us -> 4.6 us
  between operations: 14.1 us -> 0.66 us
  blocking collectives: 9.14 us -> 0 us
    reduce_scatter x1 -> x0, waiting for transfers between devices: 142 us -> none  [body(): lax.psum_scatter(filter_term, 'seq', scatter_dimension=0, tiled=True)]
    all_gather x1 -> x0, waiting for transfers between devices: 74.1 us -> none  [body(): all_taps = lax.all_gather(own_taps, 'seq', axis=0, tiled=True)]
    pallas_call x0 -> x2, Pallas kernels: none -> 49.4 us  [the longest x1 47.6 us: body(): pl.pallas_call(kernel, out_shape=(jax.ShapeDtypeStruct(blocks, BF16), jax...]
    dot_general x21 -> x0, matrix products: 40.2 us -> none  [apply_table(): jnp.dot(table, values, precision=HIGHEST, preferred_element_type=jnp.floa...]
    ppermute x8 -> x0, starting transfers between devices: 20.7 us -> none  [passed_along(): return lax.ppermute(value, axis, pairs)]
    while x40 -> x0, local copies, waits for them, and re-layouts: 15.2 us -> none
    add x13 -> x0, other arithmetic: 13.9 us -> none  [the longest x9 11.2 us: times_conj(): real_part = first_re * second_re + first_im * second_im]
    ppermute x8 -> x0, waiting for transfers between devices: 9.65 us -> none  [passed_along(): return lax.ppermute(value, axis, pairs)]
  transfers between devices with their start and end apart: 11 -> 0, of which waited for: 11 -> 0; matrix products, arithmetic and copies ran while one was open for 6% -> 0% of each run, Pallas kernels for 0% -> 0%
where the time goes in v1:
time: 54.9 us; the launch traced here: 54.6 us
  Pallas kernels  49.4 us (90%)
  local copies, waits for them, and re-layouts  4.6 us (8%)
  between operations  0.66 us (1%)
    pallas_call x1, Pallas kernels, body(): pl.pallas_call(kernel, out_shape=(jax.ShapeDtypeStruct(blocks, BF16), jax...  47.6 us
    unnamed x12, local copies, waits for them, and re-layouts  4.6 us
    pallas_call x1, Pallas kernels, body(): pl.pallas_call(finish, out_shape=(jax.ShapeDtypeStruct((TB, WIDTH), BF16)...  1.8 us

profile of v1, /device:TPU:1, one launch (start us, length us, event | category | flops | bytes accessed | tf_op | source)
XLA Modules:
  0.0 54.6 jit_solution(10442943705816948860)
XLA Ops:
  0.6 0.0 copy-start
  0.6 0.9 %copy-done = bf16[128,1024]{1,0:T(8,128)(2,1)S(1)} copy-done((bf16[128,1024]{1,0:T(8,128)(2,1)S(1)}, bf16[128,1024]{1,0:T(8,128)(2,1)}, u32[]{:S(2)}) %copy-start) | copy-done | bytes 262168
  1.6 0.0 copy-start.1
  1.6 0.9 %copy-done.1 = bf16[128,1024]{1,0:T(8,128)(2,1)S(1)} copy-done((bf16[128,1024]{1,0:T(8,128)(2,1)S(1)}, bf16[128,1024]{1,0:T(8,128)(2,1)}, u32[]{:S(2)}) %copy-start.1) | copy-done | bytes 262168
  2.5 0.0 copy-start.3
  2.5 0.8 %copy-done.3 = f32[2,4096]{1,0:T(2,128)S(1)} copy-done((f32[2,4096]{1,0:T(2,128)S(1)}, f32[2,4096]{1,0:T(2,128)}, u32[]{:S(2)}) %copy-start.3) | copy-done | bytes 32792
  3.3 0.0 copy-start.5
  3.3 0.7 %copy-done.5 = s32[32]{0:T(128)S(1)} copy-done((s32[32]{0:T(128)S(1)}, s32[32]{0:T(128)}, u32[]{:S(2)}) %copy-start.5) | copy-done | bytes 152
  3.9 47.6 %shard_map.59 = (bf16[64,16,128]{2,1,0:T(8,128)(2,1)S(1)}, f32[2,4096]{1,0:T(2,128)S(1)}) custom-call(s32[32]{0:T(128)S(1)} %copy-done.5, bf16[128,1024]{1,0:T(8,128)(2,1)S(1)} %copy-done, bf16[128,1024]{1,0:T(8,128)(2,1)S(1)} %copy-done.1, f32[2,4096]{1,0:T(2,128)S(1)} %copy-done.3), custom_call_target="tpu_custom_call" | custom-call | tf_op jit(solution)/shard_map/pallas_call | solution.py:235
  51.5 0.0 copy-start.2
  51.5 0.7 %copy-done.2 = bf16[64,16,128]{2,1,0:T(8,128)(2,1)} copy-done((bf16[64,16,128]{2,1,0:T(8,128)(2,1)}, bf16[64,16,128]{2,1,0:T(8,128)(2,1)S(1)}, u32[]{:S(2)}) %copy-start.2) | copy-done | bytes 262168
  52.2 0.0 copy-start.4
  52.2 0.6 %copy-done.4 = f32[2,4096]{1,0:T(2,128)} copy-done((f32[2,4096]{1,0:T(2,128)}, f32[2,4096]{1,0:T(2,128)S(1)}, u32[]{:S(2)}) %copy-start.4) | copy-done | bytes 32792
  52.8 1.8 %shard_map.60 = (bf16[128,1024]{1,0:T(8,128)(2,1)}, f32[2,4096]{1,0:T(2,128)}) custom-call(bf16[1024,128]{1,0:T(8,128)(2,1)} %bitcast.1, f32[2,4096]{1,0:T(2,128)} %copy-done.4), custom_call_target="tpu_custom_call" | custom-call | tf_op jit(solution)/shard_map/pallas_call | solution.py:272
Async XLA Ops:
  0.6 1.0 %copy-start = (bf16[128,1024]{1,0:T(8,128)(2,1)S(1)}, bf16[128,1024]{1,0:T(8,128)(2,1)}, u32[]{:S(2)}) copy-start(bf16[128,1024]{1,0:T(8,128)(2,1)} %grads.1) | copy-start | bytes 786436
  1.6 0.9 %copy-start.1 = (bf16[128,1024]{1,0:T(8,128)(2,1)S(1)}, bf16[128,1024]{1,0:T(8,128)(2,1)}, u32[]{:S(2)}) copy-start(bf16[128,1024]{1,0:T(8,128)(2,1)} %inputs.1) | copy-start | bytes 786436
  2.5 0.8 %copy-start.3 = (f32[2,4096]{1,0:T(2,128)S(1)}, f32[2,4096]{1,0:T(2,128)}, u32[]{:S(2)}) copy-start(f32[2,4096]{1,0:T(2,128)} %taps.1) | copy-start | bytes 98308
  3.3 0.7 %copy-start.5 = (s32[32]{0:T(128)S(1)}, s32[32]{0:T(128)}, u32[]{:S(2)}) copy-start(s32[32]{0:T(128)} %supports.1) | copy-start | bytes 388
  51.5 0.7 %copy-start.2 = (bf16[64,16,128]{2,1,0:T(8,128)(2,1)}, bf16[64,16,128]{2,1,0:T(8,128)(2,1)S(1)}, u32[]{:S(2)}) copy-start(bf16[64,16,128]{2,1,0:T(8,128)(2,1)S(1)} %get-tuple-element.4) | copy-start | bytes 786436
  52.2 0.6 %copy-start.4 = (f32[2,4096]{1,0:T(2,128)}, f32[2,4096]{1,0:T(2,128)S(1)}, u32[]{:S(2)}) copy-start(f32[2,4096]{1,0:T(2,128)S(1)} %get-tuple-element.5.gf_here) | copy-start | bytes 98308

commit v2 on v1

v2 whole, which is shorter than its diff:
```python
import functools

import jax
import jax.numpy as jnp
from jax import lax
from jax.experimental import pallas as pl
from jax.experimental.pallas import tpu as pltpu
from jax.sharding import PartitionSpec as P

MESH = pl.DeviceIdType.MESH
F32 = jnp.float32
BF16 = jnp.bfloat16
TB = 128
SMAX = 4
SEQ_DEV = 64
CHAN_DEV = 4
WIDTH = 1024
OWN = 16
LAGS = SMAX * TB
SPAN = LAGS + TB
ROWS = SEQ_DEV * OWN
NT = (((1,), (1,)), ((), ()))


def iota(shape, axis):
    return lax.broadcasted_iota(jnp.int32, shape, axis)


def high_low(value):
    high = value.astype(BF16)
    return jnp.concatenate([high, (value - high.astype(F32)).astype(BF16)], axis=0)


def take_all(landed, send_sem, recv_sem, count):
    span = landed.at[pl.ds(0, count)]
    pltpu.make_async_copy(span, span, recv_sem).wait()
    pltpu.make_async_copy(span, span, send_sem).wait()


def each_peer(me, visit):
    y, z, core = me // 16, lax.rem(me // 2, 8), lax.rem(me, 2)

    def ring(step, skip):
        far = 4 + (step + 1) // 2 * (1 - 2 * lax.rem(step, 2))
        for dy in (2, 1, 3, 0):
            chip = lax.rem(y + dy, 4) * 8 + lax.rem(z + far, 8)
            for other in (1, 0):
                if not (skip and dy == 0 and other == 0):
                    visit(chip * 2 + lax.rem(core + other, 2))
        return skip

    def one(step, carry):
        ring(step, False)
        return carry

    lax.fori_loop(0, 7, one, 0)
    ring(jnp.int32(7), True)


def spread(source, landed, send_sem, recv_sem, me):
    def one(to):
        pltpu.make_async_remote_copy(
            source.at[pl.ds(to, 1)], landed.at[pl.ds(me, 1)], send_sem, recv_sem, device_id={"seq": to}, device_id_type=MESH
        ).start()

    each_peer(me, one)


def turn(block_ref, out_ref, backwards):
    mirror = jnp.where(iota((TB, TB), 0) + iota((TB, TB), 1) == TB - 1, 1.0, 0.0).astype(BF16)
    for tile in range(WIDTH // 128):
        flipped = block_ref[:, tile * 128 : (tile + 1) * 128].astype(F32).T.astype(BF16)
        if backwards:
            flipped = jnp.dot(flipped, mirror, preferred_element_type=F32).astype(BF16)
        out_ref[tile * 8 : (tile + 1) * 8] = flipped.reshape(8, OWN, 128)


def kernel(
    supports_far, grads, inputs, taps, gi_out, gf_out,
    supports,
    g_here, x_here, t_here, g_send, x_send, g_land, x_land, gi_send,
    tap_send, tap_land, t_rows, row_send, row_land, g_wide, x_wide, gi_wide, toeplitz, windows, tap_lines, partial,
    order, back_send, back_land, last_send,
    in_sem, send_sem, recv_sem, keep_sem,
):
    me, chan = lax.axis_index("seq"), lax.axis_index("chan")
    phase = lax.rem(me, 8)
    load_g = pltpu.make_async_copy(grads, g_here, in_sem.at[0])
    load_t = pltpu.make_async_copy(taps, t_here, in_sem.at[1])
    load_x = pltpu.make_async_copy(inputs, x_here, in_sem.at[2])
    barrier = pltpu.get_barrier_semaphore()

    def greet(to):
        pl.semaphore_signal(barrier, inc=1, device_id={"seq": to}, device_id_type=MESH)

    each_peer(me, greet)
    for step in (2, 1, 3):
        pl.semaphore_signal(barrier, inc=1, device_id={"chan": lax.rem(chan + step, CHAN_DEV)}, device_id_type=MESH)
    load_s = pltpu.make_async_copy(supports_far, supports, in_sem.at[3])
    load_t.start()
    load_g.start()
    load_s.start()
    load_x.start()

    lane_group, sublane = iota((8, 128), 1) // 16, iota((8, 128), 0)
    load_t.wait()
    for x in range(CHAN_DEV):
        t_rows[2 * x : 2 * x + 2, :] = t_here[:, x * WIDTH : (x + 1) * WIDTH]
    for tile in range(8):
        block = t_rows[:, tile * 128 : (tile + 1) * 128]
        skewed = block
        for r in range(1, 8):
            skewed = jnp.where(sublane == r, pltpu.roll(block, 128 - 16 * r, axis=1), skewed)
        moved = skewed
        for k in range(1, 8):
            moved = jnp.where(lane_group == k, pltpu.roll(skewed, k, axis=0), moved)
        row_send[tile * 8 : (tile + 1) * 8, :] = moved
    row_land[pl.ds(me, 1), :] = row_send[pl.ds(me, 1), :]
    load_g.wait()
    turn(g_here, g_send, False)
    g_land[me] = g_send[me]
    load_x.wait()
    turn(x_here, x_send, True)
    x_land[me] = x_send[me]
    row = iota((512, 1), 0)
    lag_of = (row % 64) * 8 + row // 64
    order[...] = jnp.where(iota((512, LAGS), 1) == lag_of, 1.0, 0.0).astype(BF16)
    g_wide[ROWS:, :] = jnp.zeros((SMAX * OWN, 128), F32)
    load_s.wait()
    own_lags = TB * supports[chan * (WIDTH // 128) + me // 8]
    pl.semaphore_wait(barrier, SEQ_DEV - 1 + CHAN_DEV - 1)

    spread(row_send, row_land, send_sem.at[2], recv_sem.at[2], me)
    spread(g_send, g_land, send_sem.at[1], recv_sem.at[1], me)
    spread(x_send, x_land, send_sem.at[3], recv_sem.at[3], me)
    take_all(row_land, send_sem.at[2], recv_sem.at[2], SEQ_DEV - 1)
    landed = pltpu.roll(row_land[...], lax.rem(8 - phase, 8) * 16, axis=1)
    flipped = jnp.concatenate([landed, pltpu.roll(landed, 16, axis=1)], axis=0).T
    for x in range(CHAN_DEV):
        at = (8 - 2 * x) % 8 * 16
        tap_send[x] = flipped[at : at + 16]
    for step in (2, 1, 3):
        to = lax.rem(chan + step, CHAN_DEV)
        pltpu.make_async_remote_copy(
            tap_send.at[to], tap_land.at[chan], send_sem.at[0], recv_sem.at[0], device_id={"chan": to}, device_id_type=MESH
        ).start()
    tap_land[chan] = tap_send[chan]
    take_all(tap_land, send_sem.at[0], recv_sem.at[0], CHAN_DEV - 1)
    placed = jnp.concatenate([tap_land[x] for x in range(CHAN_DEV)], axis=1)
    both = jnp.dot(high_low(placed), order[...], preferred_element_type=F32)
    tap_lines[...] = jnp.where(iota((OWN, LAGS), 1) < own_lags, both[:OWN] + both[OWN:], 0.0)

    below = iota((TB, TB), 1) >= iota((TB, TB), 0)

    def build(c, carry):
        line = tap_lines[pl.ds(c, 1), :]
        before = jnp.zeros((TB, TB), F32)
        for j in range(SMAX + 1):
            if j < SMAX:
                now = jnp.broadcast_to(line[:, j * TB : (j + 1) * TB], (TB, TB))
                now = pltpu.roll(now, 0, axis=1, stride=1, stride_axis=0)
            else:
                now = jnp.zeros((TB, TB), F32)
            toeplitz[c, :, j * TB : (j + 1) * TB] = high_low(jnp.where(below, now, before))
            before = now
        return carry

    lax.fori_loop(0, OWN, build, 0, unroll=16)

    take_all(g_land, send_sem.at[1], recv_sem.at[1], SEQ_DEV - 1)
    g_wide[0:ROWS, :] = g_land[...].reshape(ROWS, 128).astype(F32)

    def signal_back(c, carry):
        for j in range(SMAX + 1):
            windows[c, :, j * TB : (j + 1) * TB] = g_wide[pl.ds(j * OWN + c, SEQ_DEV, stride=OWN), :].astype(BF16)
        both = lax.dot_general(windows[c], toeplitz[c], NT, preferred_element_type=F32)
        gi_wide[pl.ds(c, SEQ_DEV, stride=OWN), :] = both[:, :TB] + both[:, TB:]
        return carry

    lax.fori_loop(0, OWN, signal_back, 0, unroll=16)
    gi_send[...] = gi_wide[...].astype(BF16).reshape(SEQ_DEV, OWN, 128)
    spread(gi_send, gi_out, send_sem.at[4], recv_sem.at[4], me)
    keep = pltpu.make_async_copy(gi_send.at[pl.ds(me, 1)], gi_out.at[pl.ds(me, 1)], keep_sem.at[0])
    keep.start()

    take_all(x_land, send_sem.at[3], recv_sem.at[3], SEQ_DEV - 1)
    x_wide[...] = x_land[...].reshape(ROWS, 128).astype(F32)
    inside = iota((TB, TB), 1) <= iota((TB, TB), 0)

    def lag_sums(c, carry):
        signal = x_wide[pl.ds(c, SEQ_DEV, stride=OWN), :].T.astype(BF16)
        after = None
        for j in range(SMAX, -1, -1):
            product = jnp.dot(signal, windows[c, :, j * TB : (j + 1) * TB], preferred_element_type=F32)
            now = pltpu.roll(product, 1, axis=1, stride=1, stride_axis=0)
            if j < SMAX:
                lined = jnp.where(inside, now, after)
                partial[j, pl.ds(c * 8, 8), :] = jnp.sum(lined.reshape(TB // 8, 8, TB), axis=0)
            after = now
        return carry

    lax.fori_loop(0, OWN, lag_sums, 0, unroll=16)
    blocks = []
    for j in range(SMAX):
        added = partial[j, pl.ds(0, OWN, stride=8), :]
        for q in range(1, 8):
            added = added + partial[j, pl.ds(q, OWN, stride=8), :]
        blocks.append(added)
    sums = jnp.concatenate(blocks, axis=1)
    sums = jnp.where(iota((OWN, LAGS), 1) < own_lags, sums, 0.0)
    both = lax.dot_general(high_low(sums), order[...], NT, preferred_element_type=F32)
    placed = both[:OWN] + both[OWN:]
    stacked = []
    for p in range(8):
        x = (8 - p) % 8 // 2
        stacked.append(placed[:, x * 128 : (x + 1) * 128] if p % 2 == 0 else jnp.zeros((OWN, 128), F32))
    flipped = jnp.concatenate(stacked, axis=0).T
    back = flipped[:64] + pltpu.roll(flipped[64:], 112, axis=1)
    back_send[...] = pltpu.roll(back, phase * 16, axis=1)
    spread(back_send, back_land, send_sem.at[5], recv_sem.at[5], me)
    back_land[pl.ds(me, 1), :] = back_send[pl.ds(me, 1), :]
    take_all(back_land, send_sem.at[5], recv_sem.at[5], SEQ_DEV - 1)
    for tile in range(8):
        block = back_land[tile * 8 : (tile + 1) * 8, :]
        moved = block
        for k in range(1, 8):
            moved = jnp.where(lane_group == k, pltpu.roll(block, 8 - k, axis=0), moved)
        t_rows[:, tile * 128 : (tile + 1) * 128] = pltpu.roll(moved, 0, axis=1, stride=16, stride_axis=0)
    for x in range(CHAN_DEV):
        last_send[x] = t_rows[2 * x : 2 * x + 2, :]
    for step in (2, 1, 3):
        to = lax.rem(chan + step, CHAN_DEV)
        pltpu.make_async_remote_copy(
            last_send.at[to], gf_out.at[chan], send_sem.at[6], recv_sem.at[6], device_id={"chan": to}, device_id_type=MESH
        ).start()
    keep_f = pltpu.make_async_copy(last_send.at[pl.ds(chan, 1)], gf_out.at[pl.ds(chan, 1)], keep_sem.at[1])
    keep_f.start()
    take_all(gf_out, send_sem.at[6], recv_sem.at[6], CHAN_DEV - 1)
    keep_f.wait()
    keep.wait()
    take_all(gi_out, send_sem.at[4], recv_sem.at[4], SEQ_DEV - 1)


def finish(gi_rows, gf_here, gi, gf):
    for tile in range(WIDTH // 128):
        lanes = slice(tile * 128, (tile + 1) * 128)
        gi[:, lanes] = gi_rows[lanes, :].astype(F32).T.astype(BF16)
    for x in range(CHAN_DEV):
        gf[:, x * WIDTH : (x + 1) * WIDTH] = gf_here[x]


def body(inputs, grads, filter_taps, supports):
    vmem = pl.BlockSpec(memory_space=pltpu.VMEM)
    anywhere = pl.BlockSpec(memory_space=pl.ANY)
    blocks = (SEQ_DEV, OWN, 128)
    gi_rows, gf = pl.pallas_call(
        kernel,
        out_shape=(jax.ShapeDtypeStruct(blocks, BF16), jax.ShapeDtypeStruct((CHAN_DEV, 2, WIDTH), F32)),
        in_specs=[anywhere] * 4,
        out_specs=(anywhere, anywhere),
        scratch_shapes=[
            pltpu.SMEM((32,), jnp.int32),
            pltpu.VMEM((TB, WIDTH), BF16),
            pltpu.VMEM((TB, WIDTH), BF16),
            pltpu.VMEM((2, CHAN_DEV * WIDTH), F32),
            pltpu.VMEM(blocks, BF16),
            pltpu.VMEM(blocks, BF16),
            pltpu.VMEM(blocks, BF16),
            pltpu.VMEM(blocks, BF16),
            pltpu.VMEM(blocks, BF16),
            pltpu.VMEM((CHAN_DEV, OWN, 128), F32),
            pltpu.VMEM((CHAN_DEV, OWN, 128), F32),
            pltpu.VMEM((8, WIDTH), F32),
            pltpu.VMEM((SEQ_DEV, 128), F32),
            pltpu.VMEM((SEQ_DEV, 128), F32),
            pltpu.VMEM((ROWS + SMAX * OWN, 128), F32),
            pltpu.VMEM((ROWS, 128), F32),
            pltpu.VMEM((ROWS, 128), F32),
            pltpu.VMEM((OWN, 2 * TB, SPAN), BF16),
            pltpu.VMEM((OWN, SEQ_DEV, SPAN), BF16),
            pltpu.VMEM((OWN, LAGS), F32),
            pltpu.VMEM((SMAX, OWN * 8, TB), F32),
            pltpu.VMEM((512, LAGS), BF16),
            pltpu.VMEM((SEQ_DEV, 128), F32),
            pltpu.VMEM((SEQ_DEV, 128), F32),
            pltpu.VMEM((CHAN_DEV, 2, WIDTH), F32),
            pltpu.SemaphoreType.DMA((4,)),
            pltpu.SemaphoreType.DMA((7,)),
            pltpu.SemaphoreType.DMA((7,)),
            pltpu.SemaphoreType.DMA((2,)),
        ],
        compiler_params=pltpu.CompilerParams(collective_id=0, has_side_effects=True, vmem_limit_bytes=62 * 2**20),
    )(supports, grads, inputs, filter_taps)
    return pl.pallas_call(
        finish,
        out_shape=(jax.ShapeDtypeStruct((TB, WIDTH), BF16), jax.ShapeDtypeStruct((2, CHAN_DEV * WIDTH), F32)),
        in_specs=[vmem, vmem],
        out_specs=(vmem, vmem),
    )(gi_rows.reshape(ROWS, 128), gf)


def solution(mesh):
    in_specs = (P("seq", "chan"), P("seq", "chan"), P(("seq", "chan"), None), P())
    out_specs = (P("seq", "chan"), P(("seq", "chan"), None))
    return jax.shard_map(body, mesh=mesh, in_specs=in_specs, out_specs=out_specs, check_vma=False)
```

time: 54.9 us -> 41.2 us (0.75)
  Pallas kernels: 49.4 us -> 40.4 us
  local copies, waits for them, and re-layouts: 4.6 us -> 0 us
    pallas_call x1, Pallas kernels: 47.6 us -> 38.6 us  [body(): pl.pallas_call(kernel, out_shape=(jax.ShapeDtypeStruct(blocks, BF16), jax...]
    unnamed x12 -> x0, local copies, waits for them, and re-layouts: 4.6 us -> none
where the time goes in v2:
time: 41.2 us; the launch traced here: 41.1 us
  Pallas kernels  40.4 us (98%)
  between operations  0.64 us (2%)
    pallas_call x1, Pallas kernels, body(): pl.pallas_call(kernel, out_shape=(jax.ShapeDtypeStruct(blocks, BF16), jax...  38.6 us
    pallas_call x1, Pallas kernels, body(): pl.pallas_call(finish, out_shape=(jax.ShapeDtypeStruct((TB, WIDTH), BF16)...  1.8 us

profile of v2, /device:TPU:1, one launch (start us, length us, event | category | flops | bytes accessed | tf_op | source)
XLA Modules:
  0.0 41.1 jit_solution(18392961413596378930)
XLA Ops:
  0.6 38.6 %shard_map.59 = (bf16[64,16,128]{2,1,0:T(8,128)(2,1)}, f32[4,2,1024]{2,1,0:T(2,128)}) custom-call(s32[32]{0:T(128)} %supports_far.1, bf16[128,1024]{1,0:T(8,128)(2,1)} %grads.1, bf16[128,1024]{1,0:T(8,128)(2,1)} %inputs.1, f32[2,4096]{1,0:T(2,128)} %taps.1), custom_call_target="tpu_custom_call" | custom-call | tf_op jit(solution)/shard_map/pallas_call | solution.py:256
  39.3 1.8 %shard_map.60 = (bf16[128,1024]{1,0:T(8,128)(2,1)}, f32[2,4096]{1,0:T(2,128)}) custom-call(bf16[1024,128]{1,0:T(8,128)(2,1)} %bitcast.1, f32[4,2,1024]{2,1,0:T(2,128)} %get-tuple-element.5.gf_here), custom_call_target="tpu_custom_call" | custom-call | tf_op jit(solution)/shard_map/pallas_call | solution.py:294

commit v3 on v2

--- a/solution.py
+++ b/solution.py
@@ -80,7 +80,7 @@
     supports,
     g_here, x_here, t_here, g_send, x_send, g_land, x_land, gi_send,
     tap_send, tap_land, t_rows, row_send, row_land, g_wide, x_wide, gi_wide, toeplitz, windows, tap_lines, partial,
-    order, back_send, back_land, last_send,
+    order, back_send, gi_land, gi_here,
     in_sem, send_sem, recv_sem, keep_sem,
 ):
     me, chan = lax.axis_index("seq"), lax.axis_index("chan")
@@ -179,9 +179,8 @@
 
     lax.fori_loop(0, OWN, signal_back, 0, unroll=16)
     gi_send[...] = gi_wide[...].astype(BF16).reshape(SEQ_DEV, OWN, 128)
-    spread(gi_send, gi_out, send_sem.at[4], recv_sem.at[4], me)
-    keep = pltpu.make_async_copy(gi_send.at[pl.ds(me, 1)], gi_out.at[pl.ds(me, 1)], keep_sem.at[0])
-    keep.start()
+    spread(gi_send, gi_land, send_sem.at[4], recv_sem.at[4], me)
+    gi_land[me] = gi_send[me]
 
     take_all(x_land, send_sem.at[3], recv_sem.at[3], SEQ_DEV - 1)
     x_wide[...] = x_land[...].reshape(ROWS, 128).astype(F32)
@@ -217,45 +216,58 @@
     flipped = jnp.concatenate(stacked, axis=0).T
     back = flipped[:64] + pltpu.roll(flipped[64:], 112, axis=1)
     back_send[...] = pltpu.roll(back, phase * 16, axis=1)
-    spread(back_send, back_land, send_sem.at[5], recv_sem.at[5], me)
-    back_land[pl.ds(me, 1), :] = back_send[pl.ds(me, 1), :]
-    take_all(back_land, send_sem.at[5], recv_sem.at[5], SEQ_DEV - 1)
-    for tile in range(8):
-        block = back_land[tile * 8 : (tile + 1) * 8, :]
-        moved = block
-        for k in range(1, 8):
-            moved = jnp.where(lane_group == k, pltpu.roll(block, 8 - k, axis=0), moved)
-        t_rows[:, tile * 128 : (tile + 1) * 128] = pltpu.roll(moved, 0, axis=1, stride=16, stride_axis=0)
-    for x in range(CHAN_DEV):
-        last_send[x] = t_rows[2 * x : 2 * x + 2, :]
+    def to_owners(to):
+        for step in (2, 1, 3, 0):
+            other = lax.rem(chan + step, CHAN_DEV)
+            pltpu.make_async_remote_copy(
+                back_send.at[pl.ds(to, 1)], gf_out.at[pl.ds(chan * SEQ_DEV + me, 1)], send_sem.at[5], recv_sem.at[5],
+                device_id={"seq": to, "chan": other}, device_id_type=MESH,
+            ).start()
+
+    each_peer(me, to_owners)
     for step in (2, 1, 3):
-        to = lax.rem(chan + step, CHAN_DEV)
+        other = lax.rem(chan + step, CHAN_DEV)
         pltpu.make_async_remote_copy(
-            last_send.at[to], gf_out.at[chan], send_sem.at[6], recv_sem.at[6], device_id={"chan": to}, device_id_type=MESH
+            back_send.at[pl.ds(me, 1)], gf_out.at[pl.ds(chan * SEQ_DEV + me, 1)], send_sem.at[5], recv_sem.at[5],
+            device_id={"chan": other}, device_id_type=MESH,
         ).start()
-    keep_f = pltpu.make_async_copy(last_send.at[pl.ds(chan, 1)], gf_out.at[pl.ds(chan, 1)], keep_sem.at[1])
-    keep_f.start()
-    take_all(gf_out, send_sem.at[6], recv_sem.at[6], CHAN_DEV - 1)
-    keep_f.wait()
+    keep = pltpu.make_async_copy(back_send.at[pl.ds(me, 1)], gf_out.at[pl.ds(chan * SEQ_DEV + me, 1)], keep_sem.at[0])
+    keep.start()
+    take_all(gi_land, send_sem.at[4], recv_sem.at[4], SEQ_DEV - 1)
+    for tile in range(WIDTH // 128):
+        rows = gi_land[tile * 8 : (tile + 1) * 8].reshape(128, 128)
+        gi_here[:, tile * 128 : (tile + 1) * 128] = rows.astype(F32).T.astype(BF16)
+    store = pltpu.make_async_copy(gi_here, gi_out, keep_sem.at[1])
+    store.start()
     keep.wait()
-    take_all(gi_out, send_sem.at[4], recv_sem.at[4], SEQ_DEV - 1)
-
-
-def finish(gi_rows, gf_here, gi, gf):
-    for tile in range(WIDTH // 128):
-        lanes = slice(tile * 128, (tile + 1) * 128)
-        gi[:, lanes] = gi_rows[lanes, :].astype(F32).T.astype(BF16)
-    for x in range(CHAN_DEV):
-        gf[:, x * WIDTH : (x + 1) * WIDTH] = gf_here[x]
+    take_all(gf_out, send_sem.at[5], recv_sem.at[5], CHAN_DEV * SEQ_DEV - 1)
+    store.wait()
+
+
+def finish(gi_here, gf_rows, gi, gf, gf_here, sem):
+    store = pltpu.make_async_copy(gi_here, gi, sem.at[0])
+    store.start()
+    group = iota((32, 128), 1) // 16
+    for half in range(2):
+        lag = 2 * lax.axis_index("chan") + half
+        line = jnp.zeros((32, 128), F32)
+        for a in range(8):
+            line = jnp.where(group == ((a + 8 - lag) & 7), gf_rows[pl.ds(a, 32, stride=8), :], line)
+        line = pltpu.roll(line, 16 * lag, axis=1)
+        for tile in range(32):
+            gf_here[half : half + 1, tile * 128 : (tile + 1) * 128] = line[tile : tile + 1, :]
+    store_f = pltpu.make_async_copy(gf_here, gf, sem.at[1])
+    store_f.start()
+    store.wait()
+    store_f.wait()
 
 
 def body(inputs, grads, filter_taps, supports):
-    vmem = pl.BlockSpec(memory_space=pltpu.VMEM)
     anywhere = pl.BlockSpec(memory_space=pl.ANY)
     blocks = (SEQ_DEV, OWN, 128)
-    gi_rows, gf = pl.pallas_call(
+    gi, gf_rows = pl.pallas_call(
         kernel,
-        out_shape=(jax.ShapeDtypeStruct(blocks, BF16), jax.ShapeDtypeStruct((CHAN_DEV, 2, WIDTH), F32)),
+        out_shape=(pltpu.VMEM((TB, WIDTH), BF16), pltpu.VMEM((CHAN_DEV * SEQ_DEV, 128), F32)),
         in_specs=[anywhere] * 4,
         out_specs=(anywhere, anywhere),
         scratch_shapes=[
@@ -282,21 +294,23 @@
             pltpu.VMEM((SMAX, OWN * 8, TB), F32),
             pltpu.VMEM((512, LAGS), BF16),
             pltpu.VMEM((SEQ_DEV, 128), F32),
-            pltpu.VMEM((SEQ_DEV, 128), F32),
-            pltpu.VMEM((CHAN_DEV, 2, WIDTH), F32),
+            pltpu.VMEM(blocks, BF16),
+            pltpu.VMEM((TB, WIDTH), BF16),
             pltpu.SemaphoreType.DMA((4,)),
-            pltpu.SemaphoreType.DMA((7,)),
-            pltpu.SemaphoreType.DMA((7,)),
+            pltpu.SemaphoreType.DMA((6,)),
+            pltpu.SemaphoreType.DMA((6,)),
             pltpu.SemaphoreType.DMA((2,)),
         ],
-        compiler_params=pltpu.CompilerParams(collective_id=0, has_side_effects=True, vmem_limit_bytes=62 * 2**20),
-    )(supports, grads, inputs, filter_taps)
+        compiler_params=pltpu.CompilerParams(collective_id=0, has_side_effects=True, vmem_limit_bytes=48 * 2**20),
+    )(*(pltpu.with_memory_space_constraint(a, pltpu.HBM) for a in (supports, grads, inputs, filter_taps)))
     return pl.pallas_call(
         finish,
         out_shape=(jax.ShapeDtypeStruct((TB, WIDTH), BF16), jax.ShapeDtypeStruct((2, CHAN_DEV * WIDTH), F32)),
-        in_specs=[vmem, vmem],
-        out_specs=(vmem, vmem),
-    )(gi_rows.reshape(ROWS, 128), gf)
+        in_specs=[pl.BlockSpec(memory_space=pltpu.VMEM)] * 2,
+        out_specs=(anywhere, anywhere),
+        scratch_shapes=[pltpu.VMEM((2, CHAN_DEV * WIDTH), F32), pltpu.SemaphoreType.DMA((2,))],
+        compiler_params=pltpu.CompilerParams(vmem_limit_bytes=8 * 2**20),
+    )(gi, gf_rows)
 
 
 def solution(mesh):

time: 41.2 us -> 39.1 us (0.949)
  Pallas kernels: 40.4 us -> 38.3 us
    pallas_call x1, Pallas kernels: 1.8 us -> 0.74 us  [body(): pl.pallas_call(finish, out_shape=(jax.ShapeDtypeStruct((TB, WIDTH), BF16)...]
    pallas_call x1, Pallas kernels: 38.6 us -> 37.6 us  [body(): pl.pallas_call(kernel, out_shape=(pltpu.VMEM((TB, WIDTH), BF16), pltpu.VM...]
where the time goes in v3:
time: 39.1 us; the launch traced here: 39 us
  Pallas kernels  38.3 us (98%)
  between operations  0.64 us (2%)
    pallas_call x1, Pallas kernels, body(): pl.pallas_call(kernel, out_shape=(pltpu.VMEM((TB, WIDTH), BF16), pltpu.VM...  37.6 us

profile of v3, /device:TPU:1, one launch (start us, length us, event | category | flops | bytes accessed | tf_op | source)
XLA Modules:
  0.0 39.0 jit_solution(8562864881910011331)
XLA Ops:
  0.6 37.6 %shard_map.59 = (bf16[128,1024]{1,0:T(8,128)(2,1)S(1)}, f32[256,128]{1,0:T(8,128)S(1)}) custom-call(s32[32]{0:T(128)} %supports_far.1, bf16[128,1024]{1,0:T(8,128)(2,1)} %grads.1, bf16[128,1024]{1,0:T(8,128)(2,1)} %inputs.1, f32[2,4096]{1,0:T(2,128)} %taps.1), custom_call_target="tpu_custom_call" | custom-call | tf_op jit(solution)/shard_map/pallas_call | solution.py:268
  38.2 0.7 %shard_map.60 = (bf16[128,1024]{1,0:T(8,128)(2,1)}, f32[2,4096]{1,0:T(2,128)}) custom-call(bf16[128,1024]{1,0:T(8,128)(2,1)S(1)} %get-tuple-element.4.gi_here, f32[256,128]{1,0:T(8,128)S(1)} %get-tuple-element.5.gf_rows), custom_call_target="tpu_custom_call" | custom-call | tf_op jit(solution)/shard_map/pallas_call | solution.py:306

commit v4 on v3

--- a/solution.py
+++ b/solution.py
@@ -55,6 +55,21 @@
 
     lax.fori_loop(0, 7, one, 0)
     ring(jnp.int32(7), True)
+
+
+def in_order(me, visit):
+    def ring(z, carry):
+        for y in range(4):
+            for core in range(2):
+                to = (y * 8 + z) * 2 + core
+
+                @pl.when(to != me)
+                def _():
+                    visit(to)
+
+        return carry
+
+    lax.fori_loop(0, 8, ring, 0)
 
 
 def spread(source, landed, send_sem, recv_sem, me):
@@ -122,17 +137,17 @@
     load_x.wait()
     turn(x_here, x_send, True)
     x_land[me] = x_send[me]
+    pl.semaphore_wait(barrier, SEQ_DEV - 1 + CHAN_DEV - 1)
+
+    spread(row_send, row_land, send_sem.at[2], recv_sem.at[2], me)
+    spread(g_send, g_land, send_sem.at[1], recv_sem.at[1], me)
+    spread(x_send, x_land, send_sem.at[3], recv_sem.at[3], me)
     row = iota((512, 1), 0)
     lag_of = (row % 64) * 8 + row // 64
     order[...] = jnp.where(iota((512, LAGS), 1) == lag_of, 1.0, 0.0).astype(BF16)
     g_wide[ROWS:, :] = jnp.zeros((SMAX * OWN, 128), F32)
     load_s.wait()
     own_lags = TB * supports[chan * (WIDTH // 128) + me // 8]
-    pl.semaphore_wait(barrier, SEQ_DEV - 1 + CHAN_DEV - 1)
-
-    spread(row_send, row_land, send_sem.at[2], recv_sem.at[2], me)
-    spread(g_send, g_land, send_sem.at[1], recv_sem.at[1], me)
-    spread(x_send, x_land, send_sem.at[3], recv_sem.at[3], me)
     take_all(row_land, send_sem.at[2], recv_sem.at[2], SEQ_DEV - 1)
     landed = pltpu.roll(row_land[...], lax.rem(8 - phase, 8) * 16, axis=1)
     flipped = jnp.concatenate([landed, pltpu.roll(landed, 16, axis=1)], axis=0).T
@@ -224,7 +239,7 @@
                 device_id={"seq": to, "chan": other}, device_id_type=MESH,
             ).start()
 
-    each_peer(me, to_owners)
+    in_order(me, to_owners)
     for step in (2, 1, 3):
         other = lax.rem(chan + step, CHAN_DEV)
         pltpu.make_async_remote_copy(

time: 39.1 us -> 38.5 us (0.985)
  Pallas kernels: 38.3 us -> 37.8 us
    pallas_call x1, Pallas kernels: 37.6 us -> 37.1 us  [body(): pl.pallas_call(kernel, out_shape=(pltpu.VMEM((TB, WIDTH), BF16), pltpu.VM...]
where the time goes in v4:
time: 38.5 us; the launch traced here: 38.4 us
  Pallas kernels  37.8 us (98%)
  between operations  0.64 us (2%)
    pallas_call x1, Pallas kernels, body(): pl.pallas_call(kernel, out_shape=(pltpu.VMEM((TB, WIDTH), BF16), pltpu.VM...  37.1 us

profile of v4, /device:TPU:1, one launch (start us, length us, event | category | flops | bytes accessed | tf_op | source)
XLA Modules:
  0.0 38.4 jit_solution(2332975187562132705)
XLA Ops:
  0.6 37.1 %shard_map.59 = (bf16[128,1024]{1,0:T(8,128)(2,1)S(1)}, f32[256,128]{1,0:T(8,128)S(1)}) custom-call(s32[32]{0:T(128)} %supports_far.1, bf16[128,1024]{1,0:T(8,128)(2,1)} %grads.1, bf16[128,1024]{1,0:T(8,128)(2,1)} %inputs.1, f32[2,4096]{1,0:T(2,128)} %taps.1), custom_call_target="tpu_custom_call" | custom-call | tf_op jit(solution)/shard_map/pallas_call | solution.py:283
  37.7 0.7 %shard_map.60 = (bf16[128,1024]{1,0:T(8,128)(2,1)}, f32[2,4096]{1,0:T(2,128)}) custom-call(bf16[128,1024]{1,0:T(8,128)(2,1)S(1)} %get-tuple-element.4.gi_here, f32[256,128]{1,0:T(8,128)S(1)} %get-tuple-element.5.gf_rows), custom_call_target="tpu_custom_call" | custom-call | tf_op jit(solution)/shard_map/pallas_call | solution.py:321

commit v5 on v4

--- a/solution.py
+++ b/solution.py
@@ -58,14 +58,19 @@
 
 
 def in_order(me, visit):
+    y, here, core = me // 16, lax.rem(me // 2, 8), lax.rem(me, 2)
+
     def ring(z, carry):
-        for y in range(4):
-            for core in range(2):
-                to = (y * 8 + z) * 2 + core
-
-                @pl.when(to != me)
+        for dy in (2, 1, 3, 0):
+            chip = lax.rem(y + dy, 4) * 8 + z
+            visit(chip * 2 + 1 - core)
+            if dy:
+                visit(chip * 2 + core)
+            else:
+
+                @pl.when(z != here)
                 def _():
-                    visit(to)
+                    visit(chip * 2 + core)
 
         return carry
 

time: 38.5 us -> 38.6 us (level)
  no operation moved by 1% of the time
where the time goes in v5:
time: 38.6 us; the launch traced here: 38.5 us
  Pallas kernels  37.8 us (98%)
  between operations  0.64 us (2%)
    pallas_call x1, Pallas kernels, body(): pl.pallas_call(kernel, out_shape=(pltpu.VMEM((TB, WIDTH), BF16), pltpu.VM...  37.1 us

profile of v5, /device:TPU:1, one launch (start us, length us, event | category | flops | bytes accessed | tf_op | source)
XLA Modules:
  0.0 38.5 jit_solution(12282458293612765945)
XLA Ops:
  0.6 37.1 %shard_map.59 = (bf16[128,1024]{1,0:T(8,128)(2,1)S(1)}, f32[256,128]{1,0:T(8,128)S(1)}) custom-call(s32[32]{0:T(128)} %supports_far.1, bf16[128,1024]{1,0:T(8,128)(2,1)} %grads.1, bf16[128,1024]{1,0:T(8,128)(2,1)} %inputs.1, f32[2,4096]{1,0:T(2,128)} %taps.1), custom_call_target="tpu_custom_call" | custom-call | tf_op jit(solution)/shard_map/pallas_call | solution.py:288
  37.7 0.7 %shard_map.60 = (bf16[128,1024]{1,0:T(8,128)(2,1)}, f32[2,4096]{1,0:T(2,128)}) custom-call(bf16[128,1024]{1,0:T(8,128)(2,1)S(1)} %get-tuple-element.4.gi_here, f32[256,128]{1,0:T(8,128)S(1)} %get-tuple-element.5.gf_rows), custom_call_target="tpu_custom_call" | custom-call | tf_op jit(solution)/shard_map/pallas_call | solution.py:326
